TPU v7x, 32 devices: a whole 2x2x4 slice. The times are simulated.
32 devices in a mesh: owner: 8 (over y, x, core), view: 4 (over z).
Axes of the slice: x: 2, y: 2, z: 4, core: 2. Of those that a mesh axis runs over, the one named last changes fastest.
Arguments:
- first_view: bfloat16 [1472, 1024], P('owner'), may hold values from -27 to 27
- second_view: bfloat16 [1472, 1024], P(('owner', 'view')), may hold values from -6 to 6
- partner: int32 [1472], P('owner'), may hold values from 0 to 1471, each once
Outputs:
- grad_first: float32 [1472, 1024], P('owner', 'view')
- grad_second: float32 [1472, 1024], P(('owner', 'view'))
Inputs may be any that keep to these rules, and one draw needn't show every extreme that they name: partner is a permutation of the batch.
All inputs are finite; a program needn't handle non-finite values.
Results may differ from a plain program's by a relative error of at most 0.0019.
Values may be sent and summed in bfloat16 or wider, within the bound.
A program may use at most 64 MiB of HBM per device.

v0:
```python
import math

import jax
import jax.numpy as jnp
from jax import lax
from jax.sharding import PartitionSpec as P


def finish_stats(row_peak, row_mass, col_peak, col_mass):
    row_global = lax.pmax(row_peak, "view")
    row_total = lax.psum(row_mass * jnp.exp(row_peak - row_global), "view")
    col_global = lax.pmax(col_peak, "owner")
    col_total = lax.psum(col_mass * jnp.exp(col_peak - col_global), "owner")
    return (row_global + jnp.log(row_total), col_global + jnp.log(col_total))


def shards(first_view, second_view, partner):
    features = first_view.shape[1]
    shard_rows = second_view.shape[0]
    owner_count = lax.axis_size("owner")
    view_count = lax.axis_size("view")
    columns = shard_rows * owner_count
    logit_scale = 2.0 / math.sqrt(features)
    position = jnp.arange(columns, dtype=jnp.int32)
    column_ids = (
        position // shard_rows * view_count + lax.axis_index("view")
    ) * shard_rows + position % shard_rows
    target = (partner[:, None] == column_ids[None, :]).astype(jnp.float32)
    gathered = lax.all_gather(second_view, "owner", axis=0, tiled=True)
    scores = logit_scale * lax.dot_general(
        first_view, gathered, (((1,), (1,)), ((), ())), preferred_element_type=jnp.float32
    )
    row_peak = jnp.max(scores, axis=1)
    row_mass = jnp.sum(jnp.exp(scores - row_peak[:, None]), axis=1)
    col_peak = jnp.max(scores, axis=0)
    col_mass = jnp.sum(jnp.exp(scores - col_peak[None, :]), axis=0)
    row_lse, col_lse = finish_stats(row_peak, row_mass, col_peak, col_mass)
    weights = (
        0.5 * (jnp.exp(scores - row_lse[:, None]) + jnp.exp(scores - col_lse[None, :])) - target
    ).astype(jnp.bfloat16)
    grad_rows = jnp.dot(weights, gathered, preferred_element_type=jnp.float32)
    grad_first = lax.psum_scatter(logit_scale * grad_rows, "view", scatter_dimension=1, tiled=True)
    grad_second = lax.psum_scatter(
        logit_scale
        * lax.dot_general(
            weights, first_view, (((0,), (0,)), ((), ())), preferred_element_type=jnp.float32
        ),
        "owner",
        scatter_dimension=0,
        tiled=True,
    )
    return (grad_first, grad_second)


def solution(mesh):
    in_specs = (P("owner", None), P(("owner", "view"), None), P("owner"))
    out_specs = (P("owner", "view"), P(("owner", "view"), None))
    return jax.shard_map(shards, mesh=mesh, in_specs=in_specs, out_specs=out_specs, check_vma=False)
```

profile of v0, /device:TPU:4, one launch (start us, length us, event | category | flops | bytes accessed | tf_op | source)
XLA Modules:
  0.0 101.9 jit_solution(10076964738782091939)
XLA Ops:
  7.2 0.0 copy-start
  7.2 0.0 reduce-scatter.4.cloned.1.call-start
  7.2 10.5 %all-gather = bf16[8,46,1024]{2,1,0:T(8,128)(2,1)S(1)} all-gather(bf16[1,46,1024]{2,1,0:T(8,128)(2,1)} %bitcast.8), channel_id=1, replica_groups=mesh['owner'=8,'view'=4] {'owner'}, dimensions={0}, use_global_device_ids=true | all-gather | bytes 847872 | tf_op jit(solution)/shard_map/all_gather | solution.py:29
  17.7 0.0 copy-start.1
  17.8 0.2 reshape.31
  18.0 0.0 copy-done
  18.0 0.5 fusion.12
  18.5 13.2 %pmax.15 = f32[368]{0:T(512)S(1)} all-reduce(f32[368]{0:T(512)S(1)} %get-tuple-element.5), channel_id=1, replica_groups=mesh['owner'=8,'view'=4] {'owner'}, use_global_device_ids=true, to_apply=%region_5.6 | all-reduce | flops 368 | bytes 2944 | tf_op jit(solution)/shard_map/pmax | solution.py:12
  31.7 12.0 %pmax.14 = f32[184]{0:T(256)S(1)} all-reduce(f32[184]{0:T(256)S(1)} %get-tuple-element.4), channel_id=1, replica_groups=mesh['owner'=8,'view'=4] {'view'}, use_global_device_ids=true, to_apply=%region_1.2 | all-reduce | flops 184 | bytes 1472 | tf_op jit(solution)/shard_map/pmax | solution.py:10
  43.7 0.2 exponential_reduce_fusion.1
  43.9 11.8 %psum.15 = f32[368]{0:T(512)S(1)} all-reduce(f32[368]{0:T(512)S(1)} %exponential_multiply_fusion), channel_id=1, replica_groups=mesh['owner'=8,'view'=4] {'owner'}, use_global_device_ids=true, to_apply=%region_7.8 | all-reduce | flops 368 | bytes 2944 | tf_op jit(solution)/shard_map/psum | solution.py:13
  55.7 8.4 %psum.14 = f32[184]{0:T(256)S(1)} all-reduce(f32[184]{0:T(256)S(1)} %exponential_multiply_fusion.1), channel_id=1, replica_groups=mesh['owner'=8,'view'=4] {'view'}, use_global_device_ids=true, to_apply=%region_3.4 | all-reduce | flops 184 | bytes 1472 | tf_op jit(solution)/shard_map/psum | solution.py:11
  64.1 0.0 copy-done.1
  64.1 1.3 %convolution_multiply_fusion.1 = f32[184,1024]{1,0:T(8,128)} fusion(bf16[368,1024]{1,0:T(8,128)(2,1)S(1)} %reshape.31, f32[184,368]{1,0:T(8,128)S(1)} %get-tuple-element.6, s32[368]{0:T(512)S(1)} %fusion.8, f32[368]{0:T(512)S(1)} %log_add_fusion, f32[184]{0:T(256)S(1)} %log_add_fusion.1, s32[184]{0:T(256)S(1)} %copy-done.1), kind=kOutput, calls=%fused_computation.1 | convolution fusion | flops 139404288 | bytes 1782592 | tf_op jit(solution)/shard_map/dot_general | solution.py:41
  65.4 0.0 reduce-scatter.4.cloned.1.call-update
  65.4 0.0 copy-start.2
  65.4 0.5 convolution_multiply_fusion
  66.0 21.7 %fusion = f32[48,1024]{1,0:T(8,128)S(1)} fusion(f32[368,1024]{1,0:T(8,128)S(1)} %convolution_multiply_fusion), kind=kCustom, calls=%all-reduce-scatter | all-reduce-scatter fusion | flops 393217 | bytes 1704448
  87.7 1.9 %collective-permute-start = (f32[14,1024]{1,0:T(8,128)S(1)}, f32[14,1024]{1,0:T(8,128)S(1)}, u32[]{:S(2)}, u32[]{:S(2)}) collective-permute-start(f32[14,1024]{1,0:T(8,128)S(1)} %slice), channel_id=1, source_target_pairs={{0,4},{4,8},{8,12},{12,16},{16,20},{20,24},{24,28},{1,5},{5,9},{9,... | collective-permute-start | bytes 172040
  89.6 0.0 copy-done.2
  89.6 0.6 dynamic-slice.4
  90.8 3.3 %collective-permute-done = f32[14,1024]{1,0:T(8,128)S(1)} collective-permute-done((f32[14,1024]{1,0:T(8,128)S(1)}, f32[14,1024]{1,0:T(8,128)S(1)}, u32[]{:S(2)}, u32[]{:S(2)}) %collective-permute-start) | collective-permute-done | bytes 57376
  94.1 0.2 concatenate
  94.4 0.7 constant_dynamic-slice_fusion
  95.1 0.0 reduce-scatter.4.cloned.1.call-done
  (6 shorter events, 0.1 us)
Async XLA Ops:
  7.2 10.8 %copy-start = (bf16[184,1024]{1,0:T(8,128)(2,1)S(1)}, bf16[184,1024]{1,0:T(8,128)(2,1)}, u32[]{:S(2)}) copy-start(bf16[184,1024]{1,0:T(8,128)(2,1)} %param.3) | copy-start | bytes 1130500
  7.2 87.9 %reduce-scatter.4.cloned.1.call-start = ((), (), s32[]{:S(2)}) async-start(), calls=%async_computation.1 | async-start | bytes 942080 | tf_op jit(solution)/shard_map/reduce_scatter | solution.py:42
  17.7 46.3 %copy-start.1 = (s32[184]{0:T(256)S(1)}, s32[184]{0:T(256)}, u32[]{:S(2)}) copy-start(s32[184]{0:T(256)} %param.5) | copy-start | bytes 2212
  65.4 24.2 %copy-start.2 = (u32[32]{0:T(128)S(1)}, u32[32]{0:T(128)}, u32[]{:S(2)}) copy-start(u32[32]{0:T(128)} %constant.40) | copy-start | bytes 388
  87.7 6.5 %collective-permute-start = (f32[14,1024]{1,0:T(8,128)S(1)}, f32[14,1024]{1,0:T(8,128)S(1)}, u32[]{:S(2)}, u32[]{:S(2)}) collective-permute-start(f32[14,1024]{1,0:T(8,128)S(1)} %slice), channel_id=1, source_target_pairs={{0,4},{4,8},{8,12},{12,16},{16,20},{20,24},{24,28},{1,5},{5,9},{9,... | collective-permute-start | bytes 172040
Sparse Core Ops, SparseCore 0:
  65.6 21.6 reduce-scatter.3
where the time goes:
time: 102 us
  blocking collectives  77.5 us (76%)
  between operations  14.8 us (15%)
  waiting for transfers between devices  3.32 us (3%)
  matrix products  2.37 us (2%)
  starting transfers between devices  1.96 us (2%)
  local copies, waits for them, and re-layouts  1.74 us (2%)
    unnamed x1, blocking collectives  21.7 us
    pmax x1, blocking collectives, finish_stats(): col_global = lax.pmax(col_peak, 'owner')  13.2 us
    pmax x1, blocking collectives, finish_stats(): row_global = lax.pmax(row_peak, 'view')  12 us
    psum x1, blocking collectives, finish_stats(): col_total = lax.psum(col_mass * jnp.exp(col_peak - col_global), 'owner')  11.8 us
    all_gather x1, blocking collectives, shards(): gathered = lax.all_gather(second_view, 'owner', axis=0, tiled=True)  10.5 us
    psum x1, blocking collectives, finish_stats(): row_total = lax.psum(row_mass * jnp.exp(row_peak - row_global), 'view')  8.37 us
    unnamed x2, waiting for transfers between devices  3.32 us
  transfers between devices with their start and end apart: 2, of which 1 were waited for; matrix products, arithmetic and copies ran while one was open for 23% of the time, Pallas kernels for 0%

commit v1 on v0

v1 whole, which is shorter than its diff:
```python
import functools
import math

import jax
import jax.numpy as jnp
from jax import lax
from jax.experimental import pallas as pl
from jax.experimental.pallas import tpu as pltpu
from jax.sharding import PartitionSpec as P

LOW = -1e30
LANES = 128


def round_up(value, multiple):
    return (value + multiple - 1) // multiple * multiple


def kernel(
    owners, views, shard_rows,
    first_ref, second_ref, partner_ref, g1_ref, g2_ref,
    xs, fz, pbuf, wt, row_msg, col_msg, part1_send, part1_recv, merge_send, merge_recv, own2, part2_send, part2_recv,
    x_send, x_recv, xf_send, row_send, row_recv, col_send, col_recv, p1_send, p1_recv, m_send, m_recv, p2_send, p2_recv,
):
    chips = owners // 2
    rows, features = first_ref.shape
    pad = xs.shape[2]
    half = chips * pad
    columns = 2 * half
    tall = fz.shape[0]
    width = features // views
    scale = 2.0 / math.sqrt(features)
    owner = lax.axis_index("owner")
    view = lax.axis_index("view")
    chip = owner // 2
    core = owner % 2
    other = 1 - core

    def send(src, dst, send_sem, recv_sem, to_owner, to_view):
        return pltpu.make_async_remote_copy(
            src_ref=src, dst_ref=dst, send_sem=send_sem, recv_sem=recv_sem,
            device_id=(to_owner, to_view), device_id_type=pl.DeviceIdType.MESH,
        )

    barrier = pltpu.get_barrier_semaphore()
    for k in range(1, owners):
        pl.semaphore_signal(
            barrier, inc=1, device_id=((owner + k) % owners, view), device_id_type=pl.DeviceIdType.MESH
        )
    for k in range(1, views):
        pl.semaphore_signal(
            barrier, inc=1, device_id=(owner, (view + k) % views), device_id_type=pl.DeviceIdType.MESH
        )
    mine = second_ref[...]
    xs[core, chip] = jnp.concatenate([mine, jnp.zeros((pad - shard_rows, features), mine.dtype)], axis=0)
    pl.semaphore_wait(barrier, owners - 1 + views - 1)

    waits = []

    def block_send(core_of, chip_of, sems, index, to_owner):
        block = xs.at[core_of, chip_of]
        copy = send(block, block, sems.at[index], x_recv.at[core_of, chip_of], to_owner, view)
        copy.start()
        waits.append(copy)

    for k in range(1, chips):
        block_send(core, chip, x_send, k, (chip + k) % chips * 2 + core)
    block_send(core, chip, x_send, 0, chip * 2 + other)

    fz[0:rows, :] = first_ref[...]
    fz[rows:tall, :] = jnp.zeros((tall - rows, features), fz.dtype)
    pbuf[...] = jnp.zeros_like(pbuf)
    pbuf[:, 0:rows] = jnp.broadcast_to(partner_ref[...], (LANES, rows))
    partner = pbuf[...].T[0:rows]

    def block_wait(core_of, chip_of):
        block = xs.at[core_of, chip_of]
        send(block, block, x_send.at[0], x_recv.at[core_of, chip_of], owner, view).wait_recv()

    for k in range(1, chips):
        source = (chip + chips - k) % chips
        block_wait(core, source)
        block_send(core, source, xf_send, k, chip * 2 + other)
    for k in range(chips):
        block_wait(other, (chip + chips - k) % chips)

    position = lax.broadcasted_iota(jnp.int32, (1, columns), 1)
    inner = position % pad
    valid = inner < shard_rows
    slot = position // pad
    column_owner = slot % chips * 2 + slot // chips
    column_ids = jnp.where(valid, (column_owner * views + view) * shard_rows + inner, -1)
    gathered = xs[...].reshape(columns, features)
    scores = scale * lax.dot_general(
        first_ref[...], gathered, (((1,), (1,)), ((), ())), preferred_element_type=jnp.float32
    )
    scores = jnp.where(valid, scores, LOW)
    row_peak = jnp.max(scores, axis=1, keepdims=True)
    row_mass = jnp.sum(jnp.exp(scores - row_peak), axis=1, keepdims=True)
    col_peak = jnp.max(scores, axis=0, keepdims=True)
    col_mass = jnp.sum(jnp.exp(scores - col_peak), axis=0, keepdims=True)
    lane = lax.broadcasted_iota(jnp.int32, (rows, LANES), 1)
    stats = jnp.where(lane == 0, row_peak, row_mass)
    stats = jnp.concatenate([stats, jnp.zeros((tall - rows, LANES), jnp.float32)], axis=0).T
    row_msg[view, :, 0:tall] = stats[0:1]
    row_msg[view, :, tall:] = stats[1:2]
    col_msg[owner, :, 0:columns] = col_peak
    col_msg[owner, :, columns:] = col_mass
    for k in range(1, owners):
        to = (owner + k) % owners
        copy = send(col_msg.at[owner], col_msg.at[owner], col_send.at[k], col_recv.at[owner], to, view)
        copy.start()
        waits.append(copy)
    for k in range(1, views):
        to = (view + k) % views
        copy = send(row_msg.at[view], row_msg.at[view], row_send.at[k], row_recv.at[view], owner, to)
        copy.start()
        waits.append(copy)
    for k in range(1, views):
        source = (view + k) % views
        send(row_msg.at[source], row_msg.at[source], row_send.at[0], row_recv.at[source], owner, view).wait_recv()
    for k in range(1, owners):
        source = (owner + k) % owners
        send(col_msg.at[source], col_msg.at[source], col_send.at[0], col_recv.at[source], owner, view).wait_recv()

    def log_sum(msg, count, length):
        peaks = [msg[k, :, 0:length] for k in range(count)]
        peak = functools.reduce(jnp.maximum, peaks)
        mass = sum(msg[k, :, length:] * jnp.exp(peaks[k] - peak) for k in range(count))
        return peak + jnp.log(mass)

    row_lse = log_sum(row_msg, views, tall)
    col_lse = log_sum(col_msg, owners, columns)
    row_lse = jnp.broadcast_to(row_lse, (LANES, tall)).T[0:rows]
    repeat = columns // LANES
    row_lse = jnp.concatenate([row_lse] * repeat, axis=1)
    target = (jnp.concatenate([partner] * repeat, axis=1) == column_ids).astype(jnp.float32)
    weights = 0.5 * (jnp.exp(scores - row_lse) + jnp.exp(scores - col_lse)) - target

    left = weights.astype(jnp.bfloat16)

    def part1(index):
        start = pl.multiple_of(index * width, LANES)
        right = xs[:, :, :, pl.ds(start, width)].reshape(columns, width)
        return scale * jnp.dot(left, right, preferred_element_type=jnp.float32)

    for k in [2, 1, 3]:
        to = (view + k) % views
        part1_send[k, 0:rows] = part1(to).astype(jnp.bfloat16)
        copy = send(part1_send.at[k], part1_recv.at[k], p1_send.at[k], p1_recv.at[k], owner, to)
        copy.start()
        waits.append(copy)

    wide = jnp.concatenate([weights, jnp.zeros((tall - rows, columns), jnp.float32)], axis=0)
    wt[...] = wide.T.astype(jnp.bfloat16).reshape(2, half, tall)
    merge_send[...] = scale * jnp.dot(wt[other], fz[...], preferred_element_type=jnp.float32)
    merge = send(merge_send, merge_recv, m_send, m_recv, chip * 2 + other, view)
    merge.start()
    waits.append(merge)
    own2[...] = (scale * jnp.dot(wt[core], fz[...], preferred_element_type=jnp.float32))
    own1 = part1(view)
    merge.wait_recv()

    def merged(index):
        start = pl.multiple_of(index * pad, 16)
        return own2[pl.ds(start, pad), :] + merge_recv[pl.ds(start, pad), :]

    for k in range(1, chips):
        to = (chip + k) % chips
        part2_send[k] = merged(to).astype(jnp.bfloat16)
        copy = send(part2_send.at[k], part2_recv.at[k], p2_send.at[k], p2_recv.at[k], to * 2 + core, view)
        copy.start()
        waits.append(copy)
    total2 = merged(chip)
    for k in range(1, chips):
        send(part2_send.at[k], part2_recv.at[k], p2_send.at[k], p2_recv.at[k], owner, view).wait_recv()
        total2 += part2_recv[k].astype(jnp.float32)
    g2_ref[...] = total2[0:shard_rows]
    for k in range(1, views):
        send(part1_send.at[k], part1_recv.at[k], p1_send.at[k], p1_recv.at[k], owner, view).wait_recv()
        own1 += part1_recv[k, 0:rows].astype(jnp.float32)
    g1_ref[...] = own1
    for copy in waits:
        copy.wait_send()


def shards(first_view, second_view, partner):
    owners = lax.axis_size("owner")
    views = lax.axis_size("view")
    chips = owners // 2
    rows, features = first_view.shape
    shard_rows = second_view.shape[0]
    pad = round_up(shard_rows, 16)
    while 2 * chips * pad % LANES:
        pad += 16
    columns = owners * pad
    tall = round_up(rows, LANES)
    deep = round_up(rows, 16)
    width = features // views
    dma = pltpu.SemaphoreType.DMA
    vmem = pl.BlockSpec(memory_space=pltpu.VMEM)
    return pl.pallas_call(
        functools.partial(kernel, owners, views, shard_rows),
        out_shape=(
            jax.ShapeDtypeStruct((rows, width), jnp.float32),
            jax.ShapeDtypeStruct((shard_rows, features), jnp.float32),
        ),
        in_specs=[vmem] * 3,
        out_specs=(vmem, vmem),
        scratch_shapes=[
            pltpu.VMEM((2, chips, pad, features), jnp.bfloat16),
            pltpu.VMEM((tall, features), jnp.bfloat16),
            pltpu.VMEM((LANES, tall), jnp.int32),
            pltpu.VMEM((2, chips * pad, tall), jnp.bfloat16),
            pltpu.VMEM((views, 1, 2 * tall), jnp.float32),
            pltpu.VMEM((owners, 1, 2 * columns), jnp.float32),
            pltpu.VMEM((views, deep, width), jnp.bfloat16),
            pltpu.VMEM((views, deep, width), jnp.bfloat16),
            pltpu.VMEM((chips * pad, features), jnp.float32),
            pltpu.VMEM((chips * pad, features), jnp.float32),
            pltpu.VMEM((chips * pad, features), jnp.float32),
            pltpu.VMEM((chips, pad, features), jnp.bfloat16),
            pltpu.VMEM((chips, pad, features), jnp.bfloat16),
            dma((chips,)),
            dma((2, chips)),
            dma((chips,)),
            dma((views,)),
            dma((views,)),
            dma((owners,)),
            dma((owners,)),
            dma((views,)),
            dma((views,)),
            dma,
            dma,
            dma((chips,)),
            dma((chips,)),
        ],
        compiler_params=pltpu.CompilerParams(
            collective_id=0, has_side_effects=True, vmem_limit_bytes=60 * 1024 * 1024
        ),
    )(first_view, second_view, partner.reshape(1, rows))


def solution(mesh):
    in_specs = (P("owner", None), P(("owner", "view"), None), P("owner"))
    out_specs = (P("owner", "view"), P(("owner", "view"), None))
    return jax.shard_map(shards, mesh=mesh, in_specs=in_specs, out_specs=out_specs, check_vma=False)
```

time: 102 us -> 31.6 us (0.31)
  the two profiles are of different devices: /device:TPU:4 before, /device:TPU:0 now
where the time goes in v1:
time: 31.6 us; the launch traced here: 31.5 us
  Pallas kernels  28.5 us (90%)
  local copies, waits for them, and re-layouts  2.33 us (7%)
  between operations  0.65 us (2%)
    pallas_call x1, Pallas kernels, shards(): pl.pallas_call(functools.partial(kernel, owners, views, shard_rows), out_...  28.5 us
    unnamed x4, local copies, waits for them, and re-layouts  2.33 us

profile of v1, /device:TPU:0, one launch (start us, length us, event | category | flops | bytes accessed | tf_op | source)
XLA Modules:
  0.0 31.5 jit_solution(16382680249882281694)
XLA Ops:
  0.6 28.5 %shard_map.50 = (f32[184,256]{1,0:T(8,128)}, f32[46,1024]{1,0:T(8,128)}) custom-call(bf16[184,1024]{1,0:T(8,128)(2,1)} %first_ref.1, bf16[46,1024]{1,0:T(8,128)(2,1)} %second_ref.1, s32[1,184]{1,0:T(1,128)} %bitcast.1), custom_call_target="tpu_custom_call" | custom-call | tf_op jit(solution)/shard_map/pallas_call | solution.py:202
  29.1 0.0 copy-start
  29.1 1.6 %copy.7 = f32[184,256]{1,0:T(8,128)} copy(f32[184,256]{1,0:T(8,128)} %get-tuple-element.4) | data formatting | bytes 376832
  30.8 0.0 copy-done
  30.8 0.7 %copy.8 = f32[46,1024]{1,0:T(8,128)} copy(f32[46,1024]{1,0:T(8,128)S(1)} %copy-done) | data formatting | bytes 376832
Async XLA Ops:
  29.1 1.7 %copy-start = (f32[46,1024]{1,0:T(8,128)S(1)}, f32[46,1024]{1,0:T(8,128)}, u32[]{:S(2)}) copy-start(f32[46,1024]{1,0:T(8,128)} %get-tuple-element.5) | copy-start | bytes 565252

commit v2 on v1

v2 whole, which is shorter than its diff:
```python
import functools
import math

import jax
import jax.numpy as jnp
from jax import lax
from jax.experimental import pallas as pl
from jax.experimental.pallas import tpu as pltpu
from jax.sharding import PartitionSpec as P

LOW = -1e30
LANES = 128


def round_up(value, multiple):
    return (value + multiple - 1) // multiple * multiple


def kernel(
    owners, views, shard_rows,
    first_ref, second_ref, partner_ref, g1_ref, g2_ref,
    first_in, second_in, partner_in, xs, fz, pbuf, row_msg, col_msg, part1_send, part1_recv, merge_send, merge_recv, own2, part2_send, part2_recv,
    in_sem, x_send, x_recv, xf_send, row_send, row_recv, col_send, col_recv, p1_send, p1_recv, m_send, m_recv, p2_send, p2_recv,
):
    chips = owners // 2
    rows, features = first_ref.shape
    pad = xs.shape[2]
    half = chips * pad
    tall = fz.shape[0]
    width = features // views
    scale = 2.0 / math.sqrt(features)
    owner = lax.axis_index("owner")
    view = lax.axis_index("view")
    chip = owner // 2
    core = owner % 2
    other = 1 - core

    def send(src, dst, send_sem, recv_sem, to_owner, to_view):
        return pltpu.make_async_remote_copy(
            src_ref=src, dst_ref=dst, send_sem=send_sem, recv_sem=recv_sem,
            device_id=(to_owner, to_view), device_id_type=pl.DeviceIdType.MESH,
        )

    loads = [
        pltpu.make_async_copy(src, dst, in_sem.at[k])
        for k, (src, dst) in enumerate([(second_ref, second_in), (first_ref, first_in), (partner_ref, partner_in)])
    ]
    barrier = pltpu.get_barrier_semaphore()
    for k in range(1, owners):
        pl.semaphore_signal(
            barrier, inc=1, device_id=((owner + k) % owners, view), device_id_type=pl.DeviceIdType.MESH
        )
    for k in range(1, views):
        pl.semaphore_signal(
            barrier, inc=1, device_id=(owner, (view + k) % views), device_id_type=pl.DeviceIdType.MESH
        )
    for load in loads:
        load.start()
    loads[0].wait()
    mine = second_in[...]
    xs[core, chip] = jnp.concatenate([mine, jnp.zeros((pad - shard_rows, features), mine.dtype)], axis=0)
    pl.semaphore_wait(barrier, owners - 1 + views - 1)

    waits = []

    def block_send(core_of, chip_of, sems, index, to_owner):
        block = xs.at[core_of, chip_of]
        copy = send(block, block, sems.at[index], x_recv.at[core_of, chip_of], to_owner, view)
        copy.start()
        waits.append(copy)

    for k in range(1, chips):
        block_send(core, chip, x_send, k, (chip + k) % chips * 2 + core)
    block_send(core, chip, x_send, 0, chip * 2 + other)

    loads[1].wait()
    loads[2].wait()
    fz[0:rows, :] = first_in[...]
    fz[rows:tall, :] = jnp.zeros((tall - rows, features), fz.dtype)
    pbuf[...] = jnp.zeros_like(pbuf)
    pbuf[:, 0:rows] = jnp.broadcast_to(partner_in[...], (LANES, rows))
    copies = round_up(half, LANES) // LANES

    def spread(column):
        return jnp.concatenate([column] * copies, axis=1)[:, 0:half]

    partner = spread(pbuf[...].T[0:rows])
    position = lax.broadcasted_iota(jnp.int32, (1, half), 1)
    inner = position % pad
    slot = position // pad
    valid = inner < shard_rows

    def target_of(core_of):
        ids = ((slot * 2 + core_of) * views + view) * shard_rows + inner
        return (partner == jnp.where(valid, ids, -1)).astype(jnp.float32)

    sides = (core, other)
    targets = [target_of(side) for side in sides]

    def block_wait(core_of, chip_of):
        block = xs.at[core_of, chip_of]
        send(block, block, x_send.at[0], x_recv.at[core_of, chip_of], owner, view).wait_recv()

    def score(side):
        block = xs[side].reshape(half, features)
        values = scale * lax.dot_general(
            first_in[...], block, (((1,), (1,)), ((), ())), preferred_element_type=jnp.float32
        )
        return jnp.where(valid, values, LOW)

    def col_stats(side, values):
        peak = jnp.max(values, axis=0, keepdims=True)
        col_msg[owner, side, :, 0:half] = peak
        col_msg[owner, side, :, half:] = jnp.sum(jnp.exp(values - peak), axis=0, keepdims=True)

    for k in range(1, chips):
        source = (chip + chips - k) % chips
        block_wait(core, source)
        block_send(core, source, xf_send, k, chip * 2 + other)
    scores = [score(core)]
    col_stats(core, scores[0])
    for k in range(chips):
        block_wait(other, (chip + chips - k) % chips)
    scores.append(score(other))
    col_stats(other, scores[1])
    for k in range(1, owners):
        to = (owner + k) % owners
        copy = send(col_msg.at[owner], col_msg.at[owner], col_send.at[k], col_recv.at[owner], to, view)
        copy.start()
        waits.append(copy)
    row_peak = functools.reduce(jnp.maximum, [jnp.max(values, axis=1, keepdims=True) for values in scores])
    row_mass = sum(jnp.sum(jnp.exp(values - row_peak), axis=1, keepdims=True) for values in scores)
    lane = lax.broadcasted_iota(jnp.int32, (rows, LANES), 1)
    stats = jnp.where(lane == 0, row_peak, row_mass)
    stats = jnp.concatenate([stats, jnp.zeros((tall - rows, LANES), jnp.float32)], axis=0).T
    row_msg[view, :, 0:tall] = stats[0:1]
    row_msg[view, :, tall:] = stats[1:2]
    for k in range(1, views):
        to = (view + k) % views
        copy = send(row_msg.at[view], row_msg.at[view], row_send.at[k], row_recv.at[view], owner, to)
        copy.start()
        waits.append(copy)
    for k in range(1, owners):
        source = (owner + k) % owners
        send(col_msg.at[source], col_msg.at[source], col_send.at[0], col_recv.at[source], owner, view).wait_recv()

    def log_sum(parts, length):
        peaks = [part[:, 0:length] for part in parts]
        peak = functools.reduce(jnp.maximum, peaks)
        mass = sum(part[:, length:] * jnp.exp(own - peak) for part, own in zip(parts, peaks))
        return peak + jnp.log(mass)

    by_col = [
        jnp.exp(values - log_sum([col_msg[k, side] for k in range(owners)], half))
        for side, values in zip(sides, scores)
    ]
    for k in range(1, views):
        source = (view + k) % views
        send(row_msg.at[source], row_msg.at[source], row_send.at[0], row_recv.at[source], owner, view).wait_recv()
    row_lse = log_sum([row_msg[k] for k in range(views)], tall)
    row_lse = spread(jnp.broadcast_to(row_lse, (LANES, tall)).T[0:rows])
    weights = [
        0.5 * (jnp.exp(values - row_lse) + by) - target for values, by, target in zip(scores, by_col, targets)
    ]

    left = [values.astype(jnp.bfloat16) for values in weights]

    def part1(index):
        start = pl.multiple_of(index * width, LANES)
        return scale * sum(
            jnp.dot(
                values, xs[side, :, :, pl.ds(start, width)].reshape(half, width),
                preferred_element_type=jnp.float32,
            )
            for side, values in zip(sides, left)
        )

    for k in list(range(2, views)) + [1]:
        to = (view + k) % views
        part1_send[k, 0:rows] = part1(to).astype(jnp.bfloat16)
        copy = send(part1_send.at[k], part1_recv.at[k], p1_send.at[k], p1_recv.at[k], owner, to)
        copy.start()
        waits.append(copy)

    def part2(values):
        tall_values = jnp.concatenate([values, jnp.zeros((tall - rows, half), jnp.float32)], axis=0)
        return scale * jnp.dot(tall_values.T.astype(jnp.bfloat16), fz[...], preferred_element_type=jnp.float32)

    merge_send[...] = part2(weights[1])
    merge = send(merge_send, merge_recv, m_send, m_recv, chip * 2 + other, view)
    merge.start()
    waits.append(merge)
    own2[...] = part2(weights[0])
    own1 = part1(view)
    merge.wait_recv()

    def merged(index):
        start = pl.multiple_of(index * pad, 16)
        return own2[pl.ds(start, pad), :] + merge_recv[pl.ds(start, pad), :]

    for k in range(1, chips):
        to = (chip + k) % chips
        part2_send[k] = merged(to).astype(jnp.bfloat16)
        copy = send(part2_send.at[k], part2_recv.at[k], p2_send.at[k], p2_recv.at[k], to * 2 + core, view)
        copy.start()
        waits.append(copy)
    total2 = merged(chip)
    for k in range(1, chips):
        send(part2_send.at[k], part2_recv.at[k], p2_send.at[k], p2_recv.at[k], owner, view).wait_recv()
        total2 += part2_recv[k].astype(jnp.float32)
    g2_ref[...] = total2[0:shard_rows]
    for k in range(1, views):
        send(part1_send.at[k], part1_recv.at[k], p1_send.at[k], p1_recv.at[k], owner, view).wait_recv()
        own1 += part1_recv[k, 0:rows].astype(jnp.float32)
    g1_ref[...] = own1
    for copy in waits:
        copy.wait_send()


def shards(first_view, second_view, partner):
    owners = lax.axis_size("owner")
    views = lax.axis_size("view")
    chips = owners // 2
    rows, features = first_view.shape
    shard_rows = second_view.shape[0]
    pad = round_up(shard_rows, 16)
    half = chips * pad
    tall = round_up(rows, LANES)
    deep = round_up(rows, 16)
    width = features // views
    dma = pltpu.SemaphoreType.DMA
    vmem = pl.BlockSpec(memory_space=pltpu.VMEM)
    hbm = pl.BlockSpec(memory_space=pl.ANY)
    return pl.pallas_call(
        functools.partial(kernel, owners, views, shard_rows),
        out_shape=(
            pltpu.VMEM((rows, width), jnp.float32),
            pltpu.VMEM((shard_rows, features), jnp.float32),
        ),
        in_specs=[hbm] * 3,
        out_specs=(vmem, vmem),
        scratch_shapes=[
            pltpu.VMEM((rows, features), jnp.bfloat16),
            pltpu.VMEM((shard_rows, features), jnp.bfloat16),
            pltpu.VMEM((1, rows), jnp.int32),
            pltpu.VMEM((2, chips, pad, features), jnp.bfloat16),
            pltpu.VMEM((tall, features), jnp.bfloat16),
            pltpu.VMEM((LANES, tall), jnp.int32),
            pltpu.VMEM((views, 1, 2 * tall), jnp.float32),
            pltpu.VMEM((owners, 2, 1, 2 * half), jnp.float32),
            pltpu.VMEM((views, deep, width), jnp.bfloat16),
            pltpu.VMEM((views, deep, width), jnp.bfloat16),
            pltpu.VMEM((chips * pad, features), jnp.float32),
            pltpu.VMEM((chips * pad, features), jnp.float32),
            pltpu.VMEM((chips * pad, features), jnp.float32),
            pltpu.VMEM((chips, pad, features), jnp.bfloat16),
            pltpu.VMEM((chips, pad, features), jnp.bfloat16),
            dma((3,)),
            dma((chips,)),
            dma((2, chips)),
            dma((chips,)),
            dma((views,)),
            dma((views,)),
            dma((owners,)),
            dma((owners,)),
            dma((views,)),
            dma((views,)),
            dma,
            dma,
            dma((chips,)),
            dma((chips,)),
        ],
        compiler_params=pltpu.CompilerParams(
            collective_id=0, has_side_effects=True, vmem_limit_bytes=60 * 1024 * 1024
        ),
    )(first_view, second_view, partner.reshape(1, rows))


def solution(mesh):
    in_specs = (P("owner", None), P(("owner", "view"), None), P("owner"))
    out_specs = (P("owner", "view"), P(("owner", "view"), None))
    return jax.shard_map(shards, mesh=mesh, in_specs=in_specs, out_specs=out_specs, check_vma=False)
```

time: 31.6 us -> 29.1 us (0.921)
  Pallas kernels: 28.5 us -> 27 us
  local copies, waits for them, and re-layouts: 2.33 us -> 1.35 us
    pallas_call x1, Pallas kernels: 28.5 us -> 27 us  [shards(): pl.pallas_call(functools.partial(kernel, owners, views, shard_rows), out_...]
    unnamed x4 -> x2, local copies, waits for them, and re-layouts: 2.33 us -> 1.35 us
where the time goes in v2:
time: 29.1 us; the launch traced here: 28.9 us
  Pallas kernels  27 us (93%)
  local copies, waits for them, and re-layouts  1.35 us (5%)
  between operations  0.64 us (2%)
    pallas_call x1, Pallas kernels, shards(): pl.pallas_call(functools.partial(kernel, owners, views, shard_rows), out_...  27 us
    unnamed x2, local copies, waits for them, and re-layouts  1.35 us

profile of v2, /device:TPU:0, one launch (start us, length us, event | category | flops | bytes accessed | tf_op | source)
XLA Modules:
  0.0 28.9 jit_solution(8793840146512833490)
XLA Ops:
  0.6 27.0 %shard_map.50 = (f32[184,256]{1,0:T(8,128)S(1)}, f32[46,1024]{1,0:T(8,128)S(1)}) custom-call(bf16[184,1024]{1,0:T(8,128)(2,1)} %first_ref.1, bf16[46,1024]{1,0:T(8,128)(2,1)} %second_ref.1, s32[1,184]{1,0:T(1,128)} %bitcast.1), custom_call_target="tpu_custom_call" | custom-call | tf_op jit(solution)/shard_map/pallas_call | solution.py:234
  27.6 0.7 %copy.7 = f32[184,256]{1,0:T(8,128)} copy(f32[184,256]{1,0:T(8,128)S(1)} %get-tuple-element.2) | data formatting | bytes 376832
  28.3 0.7 %copy.8 = f32[46,1024]{1,0:T(8,128)} copy(f32[46,1024]{1,0:T(8,128)S(1)} %get-tuple-element.3) | data formatting | bytes 376832

commit v3 on v2

--- a/solution.py
+++ b/solution.py
@@ -113,12 +113,17 @@
         col_msg[owner, side, :, 0:half] = peak
         col_msg[owner, side, :, half:] = jnp.sum(jnp.exp(values - peak), axis=0, keepdims=True)
 
+    def row_stats(values):
+        peak = jnp.max(values, axis=1, keepdims=True)
+        return [peak, jnp.sum(jnp.exp(values - peak), axis=1, keepdims=True)]
+
     for k in range(1, chips):
         source = (chip + chips - k) % chips
         block_wait(core, source)
         block_send(core, source, xf_send, k, chip * 2 + other)
     scores = [score(core)]
     col_stats(core, scores[0])
+    row_parts = row_stats(scores[0])
     for k in range(chips):
         block_wait(other, (chip + chips - k) % chips)
     scores.append(score(other))
@@ -128,13 +133,15 @@
         copy = send(col_msg.at[owner], col_msg.at[owner], col_send.at[k], col_recv.at[owner], to, view)
         copy.start()
         waits.append(copy)
-    row_peak = functools.reduce(jnp.maximum, [jnp.max(values, axis=1, keepdims=True) for values in scores])
-    row_mass = sum(jnp.sum(jnp.exp(values - row_peak), axis=1, keepdims=True) for values in scores)
+    row_parts += row_stats(scores[1])
     lane = lax.broadcasted_iota(jnp.int32, (rows, LANES), 1)
-    stats = jnp.where(lane == 0, row_peak, row_mass)
+    stats = row_parts[3]
+    for k in (2, 1, 0):
+        stats = jnp.where(lane == k, row_parts[k], stats)
     stats = jnp.concatenate([stats, jnp.zeros((tall - rows, LANES), jnp.float32)], axis=0).T
-    row_msg[view, :, 0:tall] = stats[0:1]
-    row_msg[view, :, tall:] = stats[1:2]
+    peak = jnp.maximum(stats[0:1], stats[2:3])
+    row_msg[view, :, 0:tall] = peak
+    row_msg[view, :, tall:] = stats[1:2] * jnp.exp(stats[0:1] - peak) + stats[3:4] * jnp.exp(stats[2:3] - peak)
     for k in range(1, views):
         to = (view + k) % views
         copy = send(row_msg.at[view], row_msg.at[view], row_send.at[k], row_recv.at[view], owner, to)
@@ -175,44 +182,90 @@
             for side, values in zip(sides, left)
         )
 
-    for k in list(range(2, views)) + [1]:
-        to = (view + k) % views
-        part1_send[k, 0:rows] = part1(to).astype(jnp.bfloat16)
-        copy = send(part1_send.at[k], part1_recv.at[k], p1_send.at[k], p1_recv.at[k], owner, to)
-        copy.start()
-        waits.append(copy)
+    side = view // 2
+    parity = view % 2
+    is_end = side == parity
+    far, middle, mate = 3 * (1 - side), 2 - side, view + 1 - 2 * parity
+
+    def part1_copy(step, slot, to):
+        return send(part1_send.at[step], part1_recv.at[slot], p1_send.at[step], p1_recv.at[slot], owner, to)
+
+    def part1_start(step, slot, to):
+        copy = part1_copy(step, slot, to)
+        copy.start()
+        waits.append(copy)
+
+    def part1_wait(slot):
+        part1_copy(0, slot, mate).wait_recv()
+        return part1_recv[slot, 0:rows].astype(jnp.float32)
+
+    def pick(at_end, at_middle):
+        return jnp.where(is_end, at_end, at_middle)
+
+    part1_send[0, 0:rows] = part1(pick(far, middle)).astype(jnp.bfloat16)
+    part1_start(0, pick(0, 1 + parity), pick(mate, middle))
+    part1_send[1, 0:rows] = part1(pick(middle, mate)).astype(jnp.bfloat16)
+    part1_start(1, pick(1 + parity, 3), pick(middle, mate))
 
     def part2(values):
         tall_values = jnp.concatenate([values, jnp.zeros((tall - rows, half), jnp.float32)], axis=0)
-        return scale * jnp.dot(tall_values.T.astype(jnp.bfloat16), fz[...], preferred_element_type=jnp.float32)
+        product = scale * jnp.dot(tall_values.T.astype(jnp.bfloat16), fz[...], preferred_element_type=jnp.float32)
+        return product.reshape(chips, pad, features)
 
     merge_send[...] = part2(weights[1])
-    merge = send(merge_send, merge_recv, m_send, m_recv, chip * 2 + other, view)
-    merge.start()
-    waits.append(merge)
+
+    def merge_copy(index):
+        return send(
+            merge_send.at[index], merge_recv.at[index], m_send.at[index], m_recv.at[index], chip * 2 + other, view
+        )
+
+    order = [(chip + k) % chips for k in list(range(1, chips)) + [0]]
+    for index in order:
+        copy = merge_copy(index)
+        copy.start()
+        waits.append(copy)
     own2[...] = part2(weights[0])
+    last1 = part1(pick(mate, far))
+
+    @pl.when(is_end)
+    def _():
+        part1_send[2, 0:rows] = last1.astype(jnp.bfloat16)
+        part1_copy(2, 3, mate).start()
+
     own1 = part1(view)
-    merge.wait_recv()
 
     def merged(index):
-        start = pl.multiple_of(index * pad, 16)
-        return own2[pl.ds(start, pad), :] + merge_recv[pl.ds(start, pad), :]
+        merge_copy(index).wait_recv()
+        return own2[index] + merge_recv[index]
 
     for k in range(1, chips):
-        to = (chip + k) % chips
+        to = order[k - 1]
         part2_send[k] = merged(to).astype(jnp.bfloat16)
         copy = send(part2_send.at[k], part2_recv.at[k], p2_send.at[k], p2_recv.at[k], to * 2 + core, view)
         copy.start()
         waits.append(copy)
+
+    @pl.when(jnp.logical_not(is_end))
+    def _():
+        part1_send[2, 0:rows] = (last1 + part1_wait(0)).astype(jnp.bfloat16)
+        part1_copy(2, 0, far).start()
+
+    waits.append(part1_copy(2, 0, far))
     total2 = merged(chip)
     for k in range(1, chips):
         send(part2_send.at[k], part2_recv.at[k], p2_send.at[k], p2_recv.at[k], owner, view).wait_recv()
         total2 += part2_recv[k].astype(jnp.float32)
     g2_ref[...] = total2[0:shard_rows]
-    for k in range(1, views):
-        send(part1_send.at[k], part1_recv.at[k], p1_send.at[k], p1_recv.at[k], owner, view).wait_recv()
-        own1 += part1_recv[k, 0:rows].astype(jnp.float32)
-    g1_ref[...] = own1
+    own1 += part1_wait(3)
+
+    @pl.when(is_end)
+    def _():
+        g1_ref[...] = own1 + part1_wait(0)
+
+    @pl.when(jnp.logical_not(is_end))
+    def _():
+        g1_ref[...] = own1 + part1_wait(1) + part1_wait(2)
+
     for copy in waits:
         copy.wait_send()
 
@@ -250,9 +303,9 @@
             pltpu.VMEM((owners, 2, 1, 2 * half), jnp.float32),
             pltpu.VMEM((views, deep, width), jnp.bfloat16),
             pltpu.VMEM((views, deep, width), jnp.bfloat16),
-            pltpu.VMEM((chips * pad, features), jnp.float32),
-            pltpu.VMEM((chips * pad, features), jnp.float32),
-            pltpu.VMEM((chips * pad, features), jnp.float32),
+            pltpu.VMEM((chips, pad, features), jnp.float32),
+            pltpu.VMEM((chips, pad, features), jnp.float32),
+            pltpu.VMEM((chips, pad, features), jnp.float32),
             pltpu.VMEM((chips, pad, features), jnp.bfloat16),
             pltpu.VMEM((chips, pad, features), jnp.bfloat16),
             dma((3,)),
@@ -265,8 +318,8 @@
             dma((owners,)),
             dma((views,)),
             dma((views,)),
-            dma,
-            dma,
+            dma((chips,)),
+            dma((chips,)),
             dma((chips,)),
             dma((chips,)),
         ],

time: 29.1 us -> 29 us (level)
  no operation moved by 1% of the time
where the time goes in v3:
time: 29 us; the launch traced here: 28.8 us
  Pallas kernels  26.8 us (92%)
  local copies, waits for them, and re-layouts  1.35 us (5%)
  between operations  0.64 us (2%)
    pallas_call x1, Pallas kernels, shards(): pl.pallas_call(functools.partial(kernel, owners, views, shard_rows), out_...  26.8 us
    unnamed x2, local copies, waits for them, and re-layouts  1.35 us

profile of v3, /device:TPU:0, one launch (start us, length us, event | category | flops | bytes accessed | tf_op | source)
XLA Modules:
  0.0 28.8 jit_solution(2824458327525483510)
XLA Ops:
  0.6 26.8 %shard_map.50 = (f32[184,256]{1,0:T(8,128)S(1)}, f32[46,1024]{1,0:T(8,128)S(1)}) custom-call(bf16[184,1024]{1,0:T(8,128)(2,1)} %first_ref.1, bf16[46,1024]{1,0:T(8,128)(2,1)} %second_ref.1, s32[1,184]{1,0:T(1,128)} %bitcast.1), custom_call_target="tpu_custom_call" | custom-call | tf_op jit(solution)/shard_map/pallas_call | solution.py:287
  27.5 0.7 %copy.7 = f32[184,256]{1,0:T(8,128)} copy(f32[184,256]{1,0:T(8,128)S(1)} %get-tuple-element.2) | data formatting | bytes 376832
  28.2 0.7 %copy.8 = f32[46,1024]{1,0:T(8,128)} copy(f32[46,1024]{1,0:T(8,128)S(1)} %get-tuple-element.3) | data formatting | bytes 376832

commit v4 on v3

--- a/solution.py
+++ b/solution.py
@@ -20,7 +20,7 @@
     owners, views, shard_rows,
     first_ref, second_ref, partner_ref, g1_ref, g2_ref,
     first_in, second_in, partner_in, xs, fz, pbuf, row_msg, col_msg, part1_send, part1_recv, merge_send, merge_recv, own2, part2_send, part2_recv,
-    in_sem, x_send, x_recv, xf_send, row_send, row_recv, col_send, col_recv, p1_send, p1_recv, m_send, m_recv, p2_send, p2_recv,
+    in_sem, x_send, x_recv, xf_send, row_send, row_recv, col_send, col_recv, p1_send, p1_recv, relay_send, relay_recv, m_send, m_recv, p2_send, p2_recv,
 ):
     chips = owners // 2
     rows, features = first_ref.shape
@@ -69,8 +69,14 @@
         copy.start()
         waits.append(copy)
 
+    if chips == 4:
+        peers = [3 - chip, (chip + 2) % 4, chip + 1 - 2 * (chip % 2)]
+        sources = peers[::-1]
+    else:
+        peers = [(chip + k) % chips for k in range(1, chips)]
+        sources = [(chip + chips - k) % chips for k in range(1, chips)]
     for k in range(1, chips):
-        block_send(core, chip, x_send, k, (chip + k) % chips * 2 + core)
+        block_send(core, chip, x_send, k, peers[k - 1] * 2 + core)
     block_send(core, chip, x_send, 0, chip * 2 + other)
 
     loads[1].wait()
@@ -117,15 +123,14 @@
         peak = jnp.max(values, axis=1, keepdims=True)
         return [peak, jnp.sum(jnp.exp(values - peak), axis=1, keepdims=True)]
 
-    for k in range(1, chips):
-        source = (chip + chips - k) % chips
+    for k, source in enumerate(sources, 1):
         block_wait(core, source)
         block_send(core, source, xf_send, k, chip * 2 + other)
     scores = [score(core)]
     col_stats(core, scores[0])
     row_parts = row_stats(scores[0])
-    for k in range(chips):
-        block_wait(other, (chip + chips - k) % chips)
+    for source in [chip] + sources:
+        block_wait(other, source)
     scores.append(score(other))
     col_stats(other, scores[1])
     for k in range(1, owners):
@@ -187,25 +192,57 @@
     is_end = side == parity
     far, middle, mate = 3 * (1 - side), 2 - side, view + 1 - 2 * parity
 
+    part = part1_send.shape[1] // 2
+    spans = [(0, part), (part, rows)]
+
     def part1_copy(step, slot, to):
         return send(part1_send.at[step], part1_recv.at[slot], p1_send.at[step], p1_recv.at[slot], owner, to)
 
-    def part1_start(step, slot, to):
-        copy = part1_copy(step, slot, to)
-        copy.start()
-        waits.append(copy)
+    def relay_copy(piece, to):
+        span = pl.ds(piece * part, part)
+        return send(
+            part1_send.at[2, span], part1_recv.at[0, span], relay_send.at[piece], relay_recv.at[piece], owner, to
+        )
 
     def part1_wait(slot):
         part1_copy(0, slot, mate).wait_recv()
         return part1_recv[slot, 0:rows].astype(jnp.float32)
 
+    def relay_wait(piece):
+        relay_copy(piece, mate).wait_recv()
+        low, high = spans[piece]
+        return part1_recv[0, low:high].astype(jnp.float32)
+
     def pick(at_end, at_middle):
         return jnp.where(is_end, at_end, at_middle)
 
-    part1_send[0, 0:rows] = part1(pick(far, middle)).astype(jnp.bfloat16)
-    part1_start(0, pick(0, 1 + parity), pick(mate, middle))
-    part1_send[1, 0:rows] = part1(pick(middle, mate)).astype(jnp.bfloat16)
-    part1_start(1, pick(1 + parity, 3), pick(middle, mate))
+    def by_place(at_end, at_middle):
+        pl.when(is_end)(at_end)
+        pl.when(jnp.logical_not(is_end))(at_middle)
+
+    def middle_start(values):
+        part1_send[0, 0:rows] = values.astype(jnp.bfloat16)
+        part1_copy(0, 1 + parity, middle).start()
+
+    def mate_start(values):
+        part1_send[1, 0:rows] = values.astype(jnp.bfloat16)
+        part1_copy(1, 3, mate).start()
+
+    def relay_start(values):
+        part1_send[2, 0:rows] = values.astype(jnp.bfloat16)
+        for piece in range(2):
+            relay_copy(piece, mate).start()
+
+    def far_start(values):
+        for piece, (low, high) in enumerate(spans):
+            part1_send[2, low:high] = (values[low:high] + relay_wait(piece)).astype(jnp.bfloat16)
+            relay_copy(piece, far).start()
+
+    values1 = part1(pick(far, middle))
+    by_place(lambda: relay_start(values1), lambda: middle_start(values1))
+    values2 = part1(pick(middle, mate))
+    by_place(lambda: middle_start(values2), lambda: mate_start(values2))
+    waits += [part1_copy(0, 1, middle), part1_copy(1, 3, mate)]
 
     def part2(values):
         tall_values = jnp.concatenate([values, jnp.zeros((tall - rows, half), jnp.float32)], axis=0)
@@ -219,19 +256,14 @@
             merge_send.at[index], merge_recv.at[index], m_send.at[index], m_recv.at[index], chip * 2 + other, view
         )
 
-    order = [(chip + k) % chips for k in list(range(1, chips)) + [0]]
-    for index in order:
+    for index in peers + [chip]:
         copy = merge_copy(index)
         copy.start()
         waits.append(copy)
     own2[...] = part2(weights[0])
     last1 = part1(pick(mate, far))
 
-    @pl.when(is_end)
-    def _():
-        part1_send[2, 0:rows] = last1.astype(jnp.bfloat16)
-        part1_copy(2, 3, mate).start()
-
+    pl.when(is_end)(lambda: mate_start(last1))
     own1 = part1(view)
 
     def merged(index):
@@ -239,18 +271,14 @@
         return own2[index] + merge_recv[index]
 
     for k in range(1, chips):
-        to = order[k - 1]
+        to = peers[k - 1]
         part2_send[k] = merged(to).astype(jnp.bfloat16)
         copy = send(part2_send.at[k], part2_recv.at[k], p2_send.at[k], p2_recv.at[k], to * 2 + core, view)
         copy.start()
         waits.append(copy)
 
-    @pl.when(jnp.logical_not(is_end))
-    def _():
-        part1_send[2, 0:rows] = (last1 + part1_wait(0)).astype(jnp.bfloat16)
-        part1_copy(2, 0, far).start()
-
-    waits.append(part1_copy(2, 0, far))
+    pl.when(jnp.logical_not(is_end))(lambda: far_start(last1))
+    waits += [relay_copy(piece, far) for piece in range(2)]
     total2 = merged(chip)
     for k in range(1, chips):
         send(part2_send.at[k], part2_recv.at[k], p2_send.at[k], p2_recv.at[k], owner, view).wait_recv()
@@ -260,7 +288,8 @@
 
     @pl.when(is_end)
     def _():
-        g1_ref[...] = own1 + part1_wait(0)
+        for piece, (low, high) in enumerate(spans):
+            g1_ref[low:high] = own1[low:high] + relay_wait(piece)
 
     @pl.when(jnp.logical_not(is_end))
     def _():
@@ -318,6 +347,8 @@
             dma((owners,)),
             dma((views,)),
             dma((views,)),
+            dma((2,)),
+            dma((2,)),
             dma((chips,)),
             dma((chips,)),
             dma((chips,)),

time: 29 us -> 28.3 us (0.976)
  Pallas kernels: 26.8 us -> 26.1 us
    pallas_call x1, Pallas kernels: 26.8 us -> 26.1 us  [shards(): pl.pallas_call(functools.partial(kernel, owners, views, shard_rows), out_...]
where the time goes in v4:
time: 28.3 us; the launch traced here: 28.1 us
  Pallas kernels  26.1 us (92%)
  local copies, waits for them, and re-layouts  1.35 us (5%)
  between operations  0.64 us (2%)
    pallas_call x1, Pallas kernels, shards(): pl.pallas_call(functools.partial(kernel, owners, views, shard_rows), out_...  26.1 us
    unnamed x2, local copies, waits for them, and re-layouts  1.35 us

profile of v4, /device:TPU:0, one launch (start us, length us, event | category | flops | bytes accessed | tf_op | source)
XLA Modules:
  0.0 28.1 jit_solution(6503876903803976117)
XLA Ops:
  0.6 26.1 %shard_map.50 = (f32[184,256]{1,0:T(8,128)S(1)}, f32[46,1024]{1,0:T(8,128)S(1)}) custom-call(bf16[184,1024]{1,0:T(8,128)(2,1)} %first_ref.1, bf16[46,1024]{1,0:T(8,128)(2,1)} %second_ref.1, s32[1,184]{1,0:T(1,128)} %bitcast.1), custom_call_target="tpu_custom_call" | custom-call | tf_op jit(solution)/shard_map/pallas_call | solution.py:316
  26.8 0.7 %copy.7 = f32[184,256]{1,0:T(8,128)} copy(f32[184,256]{1,0:T(8,128)S(1)} %get-tuple-element.2) | data formatting | bytes 376832
  27.4 0.7 %copy.8 = f32[46,1024]{1,0:T(8,128)} copy(f32[46,1024]{1,0:T(8,128)S(1)} %get-tuple-element.3) | data formatting | bytes 376832

commit v5 on v4

--- a/solution.py
+++ b/solution.py
@@ -45,6 +45,8 @@
         pltpu.make_async_copy(src, dst, in_sem.at[k])
         for k, (src, dst) in enumerate([(second_ref, second_in), (first_ref, first_in), (partner_ref, partner_in)])
     ]
+    for load in loads:
+        load.start()
     barrier = pltpu.get_barrier_semaphore()
     for k in range(1, owners):
         pl.semaphore_signal(
@@ -54,8 +56,6 @@
         pl.semaphore_signal(
             barrier, inc=1, device_id=(owner, (view + k) % views), device_id_type=pl.DeviceIdType.MESH
         )
-    for load in loads:
-        load.start()
     loads[0].wait()
     mine = second_in[...]
     xs[core, chip] = jnp.concatenate([mine, jnp.zeros((pad - shard_rows, features), mine.dtype)], axis=0)

time: 28.3 us -> 28.3 us (level)
  no operation moved by 1% of the time
where the time goes in v5:
time: 28.3 us; the launch traced here: 28.1 us
  Pallas kernels  26.1 us (92%)
  local copies, waits for them, and re-layouts  1.35 us (5%)
  between operations  0.64 us (2%)
    pallas_call x1, Pallas kernels, shards(): pl.pallas_call(functools.partial(kernel, owners, views, shard_rows), out_...  26.1 us
    unnamed x2, local copies, waits for them, and re-layouts  1.35 us

profile of v5, /device:TPU:0, one launch (start us, length us, event | category | flops | bytes accessed | tf_op | source)
XLA Modules:
  0.0 28.1 jit_solution(9941317584186036706)
XLA Ops:
  0.6 26.1 %shard_map.50 = (f32[184,256]{1,0:T(8,128)S(1)}, f32[46,1024]{1,0:T(8,128)S(1)}) custom-call(bf16[184,1024]{1,0:T(8,128)(2,1)} %first_ref.1, bf16[46,1024]{1,0:T(8,128)(2,1)} %second_ref.1, s32[1,184]{1,0:T(1,128)} %bitcast.1), custom_call_target="tpu_custom_call" | custom-call | tf_op jit(solution)/shard_map/pallas_call | solution.py:316
  26.8 0.7 %copy.7 = f32[184,256]{1,0:T(8,128)} copy(f32[184,256]{1,0:T(8,128)S(1)} %get-tuple-element.2) | data formatting | bytes 376832
  27.4 0.7 %copy.8 = f32[46,1024]{1,0:T(8,128)} copy(f32[46,1024]{1,0:T(8,128)S(1)} %get-tuple-element.3) | data formatting | bytes 376832
